TPU v7x, 32 devices: a whole 2x2x4 slice. The times are simulated.
32 devices in a mesh: parts: 2 (over y), cluster: 4 (over z), tensor: 4 (over x, core).
Axes of the slice: x: 2, y: 2, z: 4, core: 2. Of those that a mesh axis runs over, the one named last changes fastest.
Arguments:
- hidden_rows: bfloat16 [128, 4096], P(('parts', 'cluster', 'tensor')), parts along dimension 0, may hold values from -5 to 5
- expert_ids: int32 [128, 2], P(('parts', 'cluster', 'tensor')), parts along dimension 0, may hold values from 0 to 3, all different within a row; in each aligned block of 4 rows (0 to 3, 4 to 7, ...) at most 2 rows name the same one
- weight_codes: int32 [128, 2], P(('parts', 'cluster', 'tensor')), parts along dimension 0, may hold values from 1 to 64
- target_rows: int32 [128], P(('parts', 'cluster', 'tensor')), parts along dimension 0, may hold values from 0 to 3, as said below
- norm_gain: float32 [4, 4096], replicated, may hold values from 0.5 to 1.5
- norm_bias: float32 [4, 4096], replicated, may hold values from -3 to 3
- head_weight: bfloat16 [4096, 131072], P(None, ('cluster', 'tensor')), may hold values from -1 to 1
Outputs:
- next_logprob: float32 [128, 32768], P(('parts', 'cluster', 'tensor')), parts along dimension 0
There are 2 independent parts, one for each index of `parts`. A program takes and returns all parts, laid end to end along the dimension named above; an argument that names none is the same for every part. Nothing has to cross between parts.
Inputs may be any that keep to these rules, and one draw needn't show every extreme that they name: `expert_ids`: A request's 2 ids differ. Among the 4 requests of one device no expert is named more than 2 times, and in some such block one expert is named exactly 2 times. `target_rows`: in each aligned block of 4 requests the entries are a permutation of 0 to 3.
All inputs are finite; a program needn't handle non-finite values.
Results may differ from a plain program's by a relative error of at most 0.0009.
Values may be sent and summed in bfloat16 or wider, within the bound.
A program may use at most 192 MiB of HBM per device.

v0:
```python
import jax
import jax.numpy as jnp
from jax import lax
from jax.sharding import PartitionSpec as P

MOST = 2


NEGATIVE = -1e30


def joined(value, axis, join):
    pieces = jax.tree.map(lambda part: lax.all_gather(part, axis), value)
    head = jax.tree.map(lambda part: part[0], pieces)
    tail = jax.tree.map(lambda part: part[1:], pieces)
    so_far, _ = lax.scan(lambda so_far, share: (join(so_far, share), None), head, tail)
    return so_far


def layer_norm(source, gain, bias):
    values = source.astype(jnp.float32)
    center = values - jnp.mean(values, axis=-1, keepdims=True)
    spread = jnp.mean(center * center, axis=-1, keepdims=True)
    return (center * lax.rsqrt(spread + 1e-05) * gain + bias).astype(jnp.bfloat16)


def combine_totals(earlier, later):
    top_first, total_first = earlier
    top_second, total_second = later
    highest = jnp.maximum(top_first, top_second)
    merged = total_first * jnp.exp(top_first - highest) + total_second * jnp.exp(
        top_second - highest
    )
    return (highest, merged)


def build_slots(slot_ids, slot_codes, slot_target, slot_source, expert, capacity, limit):
    matches = slot_ids == expert
    chosen = jnp.any(matches, axis=-1)
    code_match = jnp.sum(jnp.where(matches, slot_codes, 0), axis=-1)
    code_total = jnp.sum(slot_codes, axis=-1)
    ranking = jnp.cumsum(chosen.astype(jnp.int32), axis=-1) - 1
    places = jnp.arange(capacity, dtype=jnp.int32)
    selector = chosen[:, None, :] & (ranking[:, None, :] == places[None, :, None])
    filled = jnp.any(selector, axis=-1)
    select_int = selector.astype(jnp.int32)
    target = jnp.where(filled, jnp.sum(select_int * slot_target[:, None, :], axis=-1), limit)
    weight_code = jnp.where(filled, jnp.sum(select_int * code_match[:, None, :], axis=-1), 1)
    weight_total = jnp.where(filled, jnp.sum(select_int * code_total[:, None, :], axis=-1), 1)
    gathered = jnp.einsum(
        "smb,sbd->smd",
        selector.astype(jnp.bfloat16),
        slot_source,
        preferred_element_type=jnp.float32,
    ).astype(jnp.bfloat16)
    return (gathered, jnp.stack([target, weight_code, weight_total], axis=-1))


def local(hidden_rows, expert_ids, weight_codes, target_rows, norm_gain, norm_bias, head_weight):
    clusters = lax.axis_size("cluster")
    tensors = lax.axis_size("tensor")
    sources = clusters * tensors
    position = lax.axis_index("cluster") * tensors + lax.axis_index("tensor")
    experts = norm_gain.shape[0]
    per_expert = sources // experts
    expert = position // per_expert
    block = hidden_rows.shape[0]
    requests = block * sources
    width = head_weight.shape[1]
    capacity = MOST
    gain_row = lax.dynamic_index_in_dim(norm_gain, expert, 0, keepdims=False)
    bias_row = lax.dynamic_index_in_dim(norm_bias, expert, 0, keepdims=False)
    every_rows, every_ids, every_codes, every_target = (
        lax.all_gather(hidden_rows, ("cluster", "tensor"), axis=0, tiled=True),
        lax.all_gather(expert_ids, ("cluster", "tensor"), axis=0, tiled=True),
        lax.all_gather(weight_codes, ("cluster", "tensor"), axis=0, tiled=True),
        lax.all_gather(target_rows, ("cluster", "tensor"), axis=0, tiled=True),
    )
    block_start = (jnp.arange(sources, dtype=jnp.int32) * block)[:, None]
    global_target = every_target.reshape(sources, block) + block_start
    slot_source, slot_info = build_slots(
        every_ids.reshape(sources, block, -1),
        every_codes.reshape(sources, block, -1),
        global_target,
        every_rows.reshape(sources, block, -1),
        expert,
        capacity,
        requests,
    )
    score_slot_info = slot_info
    normed = layer_norm(slot_source, gain_row, bias_row)
    logits = jnp.einsum("smd,dv->smv", normed, head_weight, preferred_element_type=jnp.float32)
    local_top = jnp.max(logits, axis=-1)
    local_total = jnp.sum(jnp.exp(logits - local_top[..., None]), axis=-1)
    logits, local_top, local_total, slot_info = (logits, local_top, local_total, score_slot_info)
    expert_mask = (jnp.arange(experts) == expert)[:, None, None]
    spread_top = jnp.where(expert_mask, local_top[None], NEGATIVE)
    spread_total = jnp.where(expert_mask, local_total[None], 0.0)
    whole_top, whole_total = joined(
        (spread_top, spread_total), ("cluster", "tensor"), combine_totals
    )
    top_row = lax.dynamic_index_in_dim(whole_top, expert, 0, keepdims=False)
    total_row = lax.dynamic_index_in_dim(whole_total, expert, 0, keepdims=False)
    weight = slot_info[..., 1].astype(jnp.float32) / slot_info[..., 2].astype(jnp.float32)
    scores = (
        logits - top_row[..., None] - jnp.log(total_row)[..., None] + jnp.log(weight)[..., None]
    )
    flat_target = slot_info[..., 0].reshape(-1)
    outgoing = (
        jnp.full((requests, width), NEGATIVE, jnp.float32)
        .at[flat_target]
        .set(scores.reshape(-1, width), mode="drop")
    )
    outgoing = outgoing.reshape(sources, block, width)
    incoming = lax.all_to_all(
        outgoing, ("cluster", "tensor"), split_axis=0, concat_axis=0, tiled=True
    )
    grouped = incoming.reshape(experts, per_expert, block, width)
    peak = jnp.max(grouped, axis=0)
    mixed = peak + jnp.log(jnp.sum(jnp.exp(grouped - peak[None]), axis=0))
    return jnp.transpose(mixed, (1, 0, 2)).reshape(block, per_expert * width)


def solution(mesh):
    placed = (
        P(("parts", "cluster", "tensor"), None),
        P(("parts", "cluster", "tensor"), None),
        P(("parts", "cluster", "tensor"), None),
        P(("parts", "cluster", "tensor")),
        P(),
        P(),
        P(None, ("cluster", "tensor")),
    )
    return jax.shard_map(
        local,
        mesh=mesh,
        in_specs=placed,
        out_specs=P(("parts", "cluster", "tensor"), None),
        check_vma=False,
    )
```

profile of v0, /device:TPU:0, one launch (start us, length us, event | category | flops | bytes accessed | tf_op | source)
XLA Modules:
  0.0 198.1 jit_solution(12733278496266348162)
XLA Ops:
  0.0 0.0 copy-start
  0.0 23.3 %all-gather = s32[16,4,2]{1,2,0:T(2,128)S(1)} all-gather(s32[1,4,2]{1,2,0:T(2,128)} %bitcast.52), channel_id=1, replica_groups=mesh['parts'=2,'cluster'=4,'tensor'=4] {'cluster','tensor'}, dimensions={0}, use_global_device_ids=true | all-gather | bytes 544 | tf_op jit(solution)/shard_map/all_gather | solution.py:75
  23.4 0.2 reduce_window_sum.11
  23.6 0.4 fusion.11
  23.9 0.0 copy-done
  24.0 0.9 constant_dynamic-slice_fusion.1
  24.8 19.1 %all-gather.1 = bf16[16,4,4096]{2,1,0:T(4,128)(2,1)S(1)} all-gather(bf16[1,4,4096]{2,1,0:T(4,128)(2,1)} %bitcast.49), channel_id=1, replica_groups=mesh['parts'=2,'cluster'=4,'tensor'=4] {'cluster','tensor'}, dimensions={0}, use_global_device_ids=true | all-gather | bytes 557056 | tf_op jit(solution)/shard_map/all_gather | solution.py:74
  43.9 0.5 fusion.12
  44.4 0.4 multiply_reduce_fusion
  44.9 0.5 add_convert_fusion
  45.4 0.0 copy-start.3
  45.4 0.0 copy-start.2
  45.4 0.0 copy-start.1
  45.4 23.5 %fusion.13 = (f32[16,2]{0,1:T(2,128)S(1)}, f32[16,2,8192]{2,0,1:T(8,128)S(1)}) fusion(bf16[4096,8192]{1,0:T(8,128)(2,1)} %param.15, bf16[16,2,4096]{2,1,0:T(2,128)(2,1)S(1)} %add_convert_fusion), kind=kOutput, calls=%fused_computation.47 | convolution fusion | flops 2147745792 | bytes 68419712 | tf_op jit(solution)/shard_map/smd,dv->smv/dot_general | solution.py:92
  68.9 0.3 exponential_reduce_fusion.1
  69.2 0.1 broadcast_select_fusion.1
  69.3 19.0 %all_gather.24 = f32[16,4,16,2]{2,1,3,0:T(4,128)S(1)} all-gather(f32[1,4,16,2]{2,1,3,0:T(4,128)S(1)} %get-tuple-element.52), channel_id=1, replica_groups=mesh['parts'=2,'cluster'=4,'tensor'=4] {'cluster','tensor'}, dimensions={0}, use_global_device_ids=true | all-gather | bytes 8704 | tf_op jit(solution)/shard_map/all_gather | solution.py:13
  88.3 17.6 %all_gather.23 = f32[16,4,16,2]{2,1,3,0:T(4,128)S(1)} all-gather(f32[1,4,16,2]{2,1,3,0:T(4,128)S(1)} %get-tuple-element.53), channel_id=1, replica_groups=mesh['parts'=2,'cluster'=4,'tensor'=4] {'cluster','tensor'}, dimensions={0}, use_global_device_ids=true | all-gather | bytes 8704 | tf_op jit(solution)/shard_map/all_gather | solution.py:13
  105.9 0.0 copy-done.3
  105.9 0.7 dynamic-slice
  107.3 0.0 copy-done.2
  107.3 0.2 dynamic-update-slice
  107.5 9.4 %all-reduce = s32[64]{0:T(128)S(1)} all-reduce(s32[64]{0:T(128)S(1)} %dynamic-update-slice), channel_id=1, replica_groups=mesh['parts'=2,'cluster'=4,'tensor'=4] {'cluster','tensor'}, use_global_device_ids=true, to_apply=%add | all-reduce | flops 64 | bytes 512
  116.9 0.1 reshape.140
  117.0 0.1 copy.26
  117.1 0.0 copy-done.1
  117.1 20.7 %all-gather.2 = s32[16,4,2]{1,2,0:T(2,128)S(1)} all-gather(s32[1,4,2]{1,2,0:T(2,128)S(1)} %bitcast.53), channel_id=1, replica_groups=mesh['parts'=2,'cluster'=4,'tensor'=4] {'cluster','tensor'}, dimensions={0}, use_global_device_ids=true | all-gather | bytes 544 | tf_op jit(solution)/shard_map/all_gather | solution.py:76
  137.8 0.1 broadcast_add_fusion
  137.9 0.9 select_reduce_fusion.2
  138.8 0.1 copy.27
  138.8 0.1 copy.29
  138.9 0.1 select_n.80
  139.0 0.6 while.12
  139.7 0.2 subtract_add_fusion
  139.9 0.8 copy.30
  140.7 0.7 reshape.150
  141.4 1.7 scatter_custom_fusion
  143.1 1.7 reshape.143
  144.8 50.9 %all_to_all.5 = f32[16,4,8192]{2,1,0:T(4,128)S(1)} all-to-all(f32[16,4,8192]{2,1,0:T(4,128)} %reshape.143), channel_id=1, replica_groups=mesh['parts'=2,'cluster'=4,'tensor'=4] {'cluster','tensor'}, dimensions={0} | all-to-all | bytes 4194304 | tf_op jit(solution)/shard_map/all_to_all | solution.py:115
  195.7 0.7 reduce_max.19
  196.4 0.8 exponential_reduce_fusion
  197.2 0.9 log_add_fusion
  (33 shorter events, 0.6 us)
Async XLA Ops:
  0.0 23.9 %copy-start = (f32[4,4096]{1,0:T(4,128)S(1)}, f32[4,4096]{1,0:T(4,128)}, u32[]{:S(2)}) copy-start(f32[4,4096]{1,0:T(4,128)} %param.13) | copy-start | bytes 196612
  45.4 60.5 %copy-start.3 = (u32[32]{0:T(128)S(1)}, u32[32]{0:T(128)}, u32[]{:S(2)}) copy-start(u32[32]{0:T(128)} %constant.80) | copy-start | bytes 388
  45.4 61.9 %copy-start.2 = (s32[4]{0:T(128)S(1)}, s32[4]{0:T(128)}, u32[]{:S(2)}) copy-start(s32[4]{0:T(128)} %param.12) | copy-start | bytes 52
  45.4 71.7 %copy-start.1 = (s32[4,2]{0,1:T(2,128)S(1)}, s32[4,2]{0,1:T(2,128)}, u32[]{:S(2)}) copy-start(s32[4,2]{0,1:T(2,128)} %param.11) | copy-start | bytes 100
where the time goes:
time: 199 us; the launch traced here: 198 us
  blocking collectives  160 us (80%)
  matrix products  24 us (12%)
  local copies, waits for them, and re-layouts  7.14 us (4%)
  other arithmetic  5.8 us (3%)
    all_to_all x1, blocking collectives, local(): lax.all_to_all(outgoing, ('cluster', 'tensor'), split_axis=0, concat_axis...  50.9 us
    all_gather x2, blocking collectives, joined(): pieces = jax.tree.map(lambda part: lax.all_gather(part, axis), value)  36.6 us
    dot_general x1, matrix products, local(): jnp.einsum('smd,dv->smv', normed, head_weight, preferred_element_type=jnp...  23.5 us
    all_gather x1, blocking collectives, local(): lax.all_gather(expert_ids, ('cluster', 'tensor'), axis=0, tiled=True)  23.3 us
    all_gather x1, blocking collectives, local(): lax.all_gather(weight_codes, ('cluster', 'tensor'), axis=0, tiled=True)  20.7 us
    all_gather x1, blocking collectives, local(): lax.all_gather(hidden_rows, ('cluster', 'tensor'), axis=0, tiled=True)  19.1 us
    unnamed x1, blocking collectives  9.39 us

commit v1 on v0

v1 whole, which is shorter than its diff:
```python
import functools

import jax
import jax.numpy as jnp
from jax import lax
from jax.experimental import pallas as pl
from jax.experimental.pallas import tpu as pltpu
from jax.sharding import PartitionSpec as P

MOST = 2
LANES = 128
NEGATIVE = -1e30
CHUNK = 512
GROUP = 1024
SLOTS = 12
STEPS = 32000.0
VMEM_BYTES = 60 * 2**20


def kernel(
    experts, ids, codes, target, hidden, gain, bias, weight, out,
    hidden_v, gain_v, bias_v, rows3, gain3, bias3, picked, arrived, wide, lhs, held,
    natural, coded, quant, landed, stats, stat_out, stat_in, offsets,
    small_sem, held_sem, row_send, row_recv, data_send, data_recv, stat_send, stat_recv,
):
    clusters = lax.axis_size("cluster")
    tensors = lax.axis_size("tensor")
    sources = clusters * tensors
    per = sources // experts
    me = lax.axis_index("cluster") * tensors + lax.axis_index("tensor")
    mine = me // per
    block, topk = ids.shape
    depth = hidden.shape[1]
    width = weight.shape[1]
    groups = width // GROUP
    chunks = width // CHUNK
    parts = GROUP // CHUNK
    slots = held.shape[0]
    tall = GROUP // LANES
    rows = MOST * sources

    def device(p):
        return {"cluster": p // tensors, "tensor": lax.rem(p, tensors)}

    def other(i):
        return lax.rem(me + i, sources)

    def fetch(c, slot):
        return pltpu.make_async_copy(
            weight.at[:, pl.ds(pl.multiple_of(c * CHUNK, CHUNK), CHUNK)],
            held.at[slot],
            held_sem.at[slot],
        )

    small = [
        pltpu.make_async_copy(src, dst, small_sem.at[i])
        for i, (src, dst) in enumerate(((hidden, hidden_v), (gain, gain_v), (bias, bias_v)))
    ]
    for copy in small:
        copy.start()
    for c in range(slots):
        fetch(c, c).start()

    barrier = pltpu.get_barrier_semaphore()

    @pl.loop(1, sources)
    def _(i):
        pl.semaphore_signal(
            barrier, inc=1, device_id=device(other(i)), device_id_type=pl.DeviceIdType.MESH
        )

    for copy in small:
        copy.wait()
    values = hidden_v[...].astype(jnp.float32)
    center = values - jnp.mean(values, axis=-1, keepdims=True)
    spread = jnp.mean(center * center, axis=-1, keepdims=True)
    scaled = center * lax.rsqrt(spread + 1e-05)
    for k in range(depth // LANES):
        part = slice(k * LANES, (k + 1) * LANES)
        rows3[:, k, :] = scaled[:, part]
        gain3[:, k, :] = gain_v[:, part]
        bias3[:, k, :] = bias_v[:, part]

    def names(r, e):
        hit = ids[r, 0] == e
        for k in range(1, topk):
            hit = hit | (ids[r, k] == e)
        return hit.astype(jnp.int32)

    for e in range(experts):
        for m in range(MOST):
            row, rank = jnp.int32(0), jnp.int32(0)
            for r in range(block):
                hit = names(r, e)
                row = row + jnp.where(rank == m, hit * r, 0)
                rank = rank + hit
            picked[e, m] = (rows3[row] * gain3[e] + bias3[e]).astype(jnp.bfloat16)

    pl.semaphore_wait(barrier, sources - 1)

    @pl.loop(1, sources)
    def _(i):
        p = other(i)
        pltpu.make_async_remote_copy(
            picked.at[p // per], arrived.at[me], row_send, row_recv,
            device_id=device(p), device_id_type=pl.DeviceIdType.MESH,
        ).start()

    pltpu.make_async_copy(picked.at[mine], arrived.at[me], row_recv).start()
    lane = lax.broadcasted_iota(jnp.int32, (rows, LANES), 1)
    stats[0] = jnp.full((rows, LANES), NEGATIVE, jnp.float32)
    for q in range(1, 4):
        stats[q] = jnp.zeros((rows, LANES), jnp.float32)
    for q in range(4, 8):
        stat_out[:, q, :] = jnp.zeros((rows, LANES), jnp.float32)
    pltpu.make_async_copy(arrived, arrived, row_recv).wait()
    wide[...] = arrived[...].astype(jnp.float32).reshape(wide.shape)
    for k in range(depth // LANES):
        lhs[:, k * LANES:(k + 1) * LANES] = wide[:, k, :].astype(jnp.bfloat16)

    def wait_send(g):
        gone = quant.at[g, pl.ds(0, sources - 1)]
        pltpu.make_async_copy(gone, gone, data_send.at[g]).wait()

    def wait_recv(g):
        pltpu.make_async_copy(landed.at[g], landed.at[g], data_recv.at[g]).wait()

    @pl.loop(0, groups)
    def _(g):
        for h in range(parts):
            c = g * parts + h
            slot = lax.rem(c, slots)
            fetch(c, slot).wait()
            natural[:, h * CHUNK:(h + 1) * CHUNK] = jnp.dot(
                lhs[...], held[slot], preferred_element_type=jnp.float32
            )

            @pl.when(c + slots < chunks)
            def _():
                fetch(c + slots, slot).start()

        pieces = [natural[:, j * LANES:(j + 1) * LANES] for j in range(tall)]
        top = jnp.max(functools.reduce(jnp.maximum, pieces), axis=1, keepdims=True)
        low = jnp.min(functools.reduce(jnp.minimum, pieces), axis=1, keepdims=True)
        middle = 0.5 * top + 0.5 * low
        half = jnp.maximum(top - middle, 1e-20)
        inverse = STEPS / half
        total = jnp.zeros((rows, LANES), jnp.float32)
        for j, piece in enumerate(pieces):
            coded[:, j, :] = jnp.round((piece - middle) * inverse)
            total = total + jnp.exp(piece - top)
        total = jnp.sum(total, axis=1, keepdims=True)
        quant[g] = coded[...].reshape(sources, MOST * tall, LANES).astype(jnp.int32).astype(jnp.int16)
        for q, value in enumerate((top, total, middle, half / STEPS)):
            stats[q] = jnp.where(lane == g, value, stats[q])

        @pl.loop(1, sources)
        def _(i):
            p = other(i)
            pltpu.make_async_remote_copy(
                quant.at[g, p], landed.at[g, me], data_send.at[g], data_recv.at[g],
                device_id=device(p), device_id_type=pl.DeviceIdType.MESH,
            ).start()

        pltpu.make_async_copy(quant.at[g, me], landed.at[g, me], data_recv.at[g]).start()

    for q in range(4):
        stat_out[:, q, :] = stats[q]

    @pl.loop(1, sources)
    def _(i):
        p = other(i)
        pltpu.make_async_remote_copy(
            stat_out.at[pl.ds(MOST * p, MOST)], stat_in.at[me], stat_send, stat_recv,
            device_id=device(p), device_id_type=pl.DeviceIdType.MESH,
        ).start()

    pltpu.make_async_copy(
        stat_out.at[pl.ds(MOST * me, MOST)], stat_in.at[me], stat_recv
    ).start()
    gone_rows = arrived.at[pl.ds(0, sources - 1)]
    pltpu.make_async_copy(gone_rows, gone_rows, row_send).wait()
    pltpu.make_async_copy(stat_in, stat_in, stat_recv).wait()
    for e in range(experts):
        for m in range(MOST):
            owned = slice(e * per, (e + 1) * per)
            tops = stat_in[owned, m, 0, :]
            highest = jnp.max(tops, keepdims=True)
            whole = jnp.sum(stat_in[owned, m, 1, :] * jnp.exp(tops - highest), keepdims=True)
            offsets[e * MOST + m] = (stat_in[owned, m, 2, :] - highest) - jnp.log(whole)

    @pl.loop(0, groups)
    def _(g):
        wait_recv(g)
        wait_send(g)

    for t in range(block):
        r = jnp.int32(0)
        for other_row in range(block):
            r = jnp.where(target[other_row] == t, other_row, r)
        code_total = codes[r, 0]
        for k in range(1, topk):
            code_total = code_total + codes[r, k]
        code_total = jnp.full((1, LANES), code_total, jnp.int32).astype(jnp.float32)
        named = []
        for k in range(topk):
            e = ids[r, k]
            m = jnp.int32(0)
            for other_row in range(block):
                m = m + jnp.where(other_row < r, names(other_row, e), 0)
            m = jnp.minimum(m, MOST - 1)
            share = jnp.full((1, LANES), codes[r, k], jnp.int32).astype(jnp.float32) / code_total
            named.append((e, m, jnp.log(share)))

        @pl.loop(0, per)
        def _(j):
            loaded = []
            for e, m, log_share in named:
                step = stat_in[e * per + j, m][3:4]
                offset = offsets[e * MOST + m, pl.ds(j, 1)] + log_share
                loaded.append((e * per + j, m, step, offset))
            for g in range(groups):
                scores = []
                for source, m, step, offset in loaded:
                    tile = landed[g, source].astype(jnp.int32).astype(jnp.float32)
                    tile = jnp.where(m == 0, tile[:tall], tile[tall:])
                    scores.append(tile * step[:, g:g + 1] + offset[:, g:g + 1])
                peak = functools.reduce(jnp.maximum, scores)
                summed = sum(jnp.exp(score - peak) for score in scores)
                place = pl.multiple_of((j * groups + g) * tall, tall)
                out[pl.ds(place, tall), t, :] = peak + jnp.log(summed)

    gone_stats = stat_out.at[pl.ds(0, MOST * (sources - 1))]
    pltpu.make_async_copy(gone_stats, gone_stats, stat_send).wait()


def local(hidden_rows, expert_ids, weight_codes, target_rows, norm_gain, norm_bias, head_weight):
    sources = lax.axis_size("cluster") * lax.axis_size("tensor")
    experts, depth = norm_gain.shape
    block = hidden_rows.shape[0]
    width = head_weight.shape[1]
    per = sources // experts
    rows = MOST * sources
    groups, chunks = width // GROUP, width // CHUNK
    tall = GROUP // LANES
    slots = min(SLOTS, chunks)
    high = depth // LANES
    f32, bf16 = jnp.float32, jnp.bfloat16
    scratch = [
        pltpu.VMEM((block, depth), bf16),
        pltpu.VMEM((experts, depth), f32),
        pltpu.VMEM((experts, depth), f32),
        pltpu.VMEM((block, high, LANES), f32),
        pltpu.VMEM((experts, high, LANES), f32),
        pltpu.VMEM((experts, high, LANES), f32),
        pltpu.VMEM((experts, MOST, high, LANES), bf16),
        pltpu.VMEM((sources, MOST, high, LANES), bf16),
        pltpu.VMEM((rows, high, LANES), f32),
        pltpu.VMEM((rows, depth), bf16),
        pltpu.VMEM((slots, depth, CHUNK), bf16),
        pltpu.VMEM((rows, GROUP), f32),
        pltpu.VMEM((rows, tall, LANES), f32),
        pltpu.VMEM((groups, sources, MOST * tall, LANES), jnp.int16),
        pltpu.VMEM((groups, sources, MOST * tall, LANES), jnp.int16),
        pltpu.VMEM((4, rows, LANES), f32),
        pltpu.VMEM((rows, 8, LANES), f32),
        pltpu.VMEM((sources, MOST, 8, LANES), f32),
        pltpu.VMEM((experts * MOST, per, LANES), f32),
        pltpu.SemaphoreType.DMA((3,)),
        pltpu.SemaphoreType.DMA((slots,)),
        pltpu.SemaphoreType.DMA,
        pltpu.SemaphoreType.DMA,
        pltpu.SemaphoreType.DMA((groups,)),
        pltpu.SemaphoreType.DMA((groups,)),
        pltpu.SemaphoreType.DMA,
        pltpu.SemaphoreType.DMA,
    ]
    smem = pl.BlockSpec(memory_space=pltpu.SMEM)
    anywhere = pl.BlockSpec(memory_space=pl.ANY)
    mixed = pl.pallas_call(
        functools.partial(kernel, experts),
        out_shape=jax.ShapeDtypeStruct((per * width // LANES, block, LANES), f32),
        in_specs=[smem] * 3 + [anywhere] * 4,
        out_specs=pl.BlockSpec(memory_space=pltpu.VMEM),
        scratch_shapes=scratch,
        compiler_params=pltpu.CompilerParams(
            collective_id=0, has_side_effects=True, vmem_limit_bytes=VMEM_BYTES
        ),
        cost_estimate=pl.CostEstimate(
            flops=2 * rows * depth * width,
            bytes_accessed=2 * depth * width,
            transcendentals=3 * rows * width,
        ),
    )(expert_ids, weight_codes, target_rows, hidden_rows, norm_gain, norm_bias, head_weight)
    return jnp.transpose(mixed, (1, 0, 2)).reshape(block, per * width)


def solution(mesh):
    rows = P(("parts", "cluster", "tensor"), None)
    placed = (
        rows,
        rows,
        rows,
        P(("parts", "cluster", "tensor")),
        P(),
        P(),
        P(None, ("cluster", "tensor")),
    )
    return jax.shard_map(
        local, mesh=mesh, in_specs=placed, out_specs=rows, check_vma=False
    )
```

time: 199 us -> 58.1 us (0.29)
  blocking collectives: 160 us -> 0 us
  Pallas kernels: 0 us -> 53.3 us
  matrix products: 24 us -> 0 us
  other arithmetic: 5.8 us -> 0 us
  local copies, waits for them, and re-layouts: 7.14 us -> 4.55 us
    all_gather x5 -> x0, blocking collectives: 99.7 us -> none  [the longest x2 36.6 us: joined(): pieces = jax.tree.map(lambda part: lax.all_gather(part, axis), value)]
    pallas_call x0 -> x1, Pallas kernels: none -> 53.3 us  [local(): pl.pallas_call(functools.partial(kernel, experts), out_shape=jax.ShapeDty...]
    all_to_all x1 -> x0, blocking collectives: 50.9 us -> none  [local(): lax.all_to_all(outgoing, ('cluster', 'tensor'), split_axis=0, concat_axis...]
    dot_general x2 -> x0, matrix products: 24 us -> none  [the longest x1 23.5 us: local(): jnp.einsum('smd,dv->smv', normed, head_weight, preferred_element_type=jnp...]
    unnamed x1 -> x0, blocking collectives: 9.39 us -> none
    unnamed x11 -> x3, local copies, waits for them, and re-layouts: 0.93 us -> 4.55 us
    reshape x3 -> x0, local copies, waits for them, and re-layouts: 2.48 us -> none  [the longest x1 1.68 us: local(): outgoing = outgoing.reshape(sources, block, width)]
    reduce_sum x5 -> x0, other arithmetic: 2.47 us -> none  [the longest x1 0.89 us: build_slots(): jnp.sum(select_int * code_match[:, None, :], axis=-1)]
where the time goes in v1:
time: 58.1 us; the launch traced here: 57.8 us
  Pallas kernels  53.3 us (92%)
  local copies, waits for them, and re-layouts  4.55 us (8%)
    pallas_call x1, Pallas kernels, local(): pl.pallas_call(functools.partial(kernel, experts), out_shape=jax.ShapeDty...  53.3 us
    unnamed x3, local copies, waits for them, and re-layouts  4.55 us

profile of v1, /device:TPU:0, one launch (start us, length us, event | category | flops | bytes accessed | tf_op | source)
XLA Modules:
  0.0 57.8 jit_solution(7151879912008314890)
XLA Ops:
  0.0 1.3 %copy.8.ids = s32[4,2]{1,0:T(4,128)} copy(s32[4,2]{0,1:T(2,128)} %param.8) | data formatting | bytes 64 | tf_op args[1]
  1.3 1.4 %copy.9.codes = s32[4,2]{1,0:T(4,128)} copy(s32[4,2]{0,1:T(2,128)} %param.9) | data formatting | bytes 64 | tf_op args[2]
  2.7 53.3 %shard_map.73 = f32[256,4,128]{2,1,0:T(4,128)} custom-call(s32[4,2]{1,0:T(4,128)} %copy.8.ids, s32[4,2]{1,0:T(4,128)} %copy.9.codes, s32[4]{0:T(128)} %target.1, bf16[4,4096]{1,0:T(4,128)(2,1)} %hidden.1, f32[4,4096]{1,0:T(4,128)} %gain.1, f32[4,4096]{1,0:T(4,128)} %bias.1, bf16[4096,8192]{1,0:T(8,128)(2,1)} %weight.1), custom_call_target="tpu_custom_call" | custom-call | flops 2147483648 | bytes 67108864 | tf_op jit(solution)/shard_map/pallas_call | solution.py:280
  56.0 1.9 %copy.11 = f32[4,32768]{1,0:T(4,128)} copy(f32[4,32768]{1,0:T(4,128)} %bitcast.3) | data formatting | bytes 1048576

commit v2 on v1

--- a/solution.py
+++ b/solution.py
@@ -13,6 +13,7 @@
 CHUNK = 512
 GROUP = 1024
 SLOTS = 12
+EARLY = 4
 STEPS = 32000.0
 VMEM_BYTES = 60 * 2**20
 
@@ -21,7 +22,7 @@
     experts, ids, codes, target, hidden, gain, bias, weight, out,
     hidden_v, gain_v, bias_v, rows3, gain3, bias3, picked, arrived, wide, lhs, held,
     natural, coded, quant, landed, stats, stat_out, stat_in, offsets,
-    small_sem, held_sem, row_send, row_recv, data_send, data_recv, stat_send, stat_recv,
+    small_sem, held_sem, row_send, row_recv, pass_send, pass_recv, data_send, data_recv, stat_send, stat_recv,
 ):
     clusters = lax.axis_size("cluster")
     tensors = lax.axis_size("tensor")
@@ -29,7 +30,8 @@
     per = sources // experts
     me = lax.axis_index("cluster") * tensors + lax.axis_index("tensor")
     mine = me // per
-    block, topk = ids.shape
+    topk, block = ids.shape
+    spot = lax.rem(me, per)
     depth = hidden.shape[1]
     width = weight.shape[1]
     groups = width // GROUP
@@ -58,7 +60,8 @@
     ]
     for copy in small:
         copy.start()
-    for c in range(slots):
+    early = min(EARLY, slots)
+    for c in range(early):
         fetch(c, c).start()
 
     barrier = pltpu.get_barrier_semaphore()
@@ -82,9 +85,9 @@
         bias3[:, k, :] = bias_v[:, part]
 
     def names(r, e):
-        hit = ids[r, 0] == e
+        hit = ids[0, r] == e
         for k in range(1, topk):
-            hit = hit | (ids[r, k] == e)
+            hit = hit | (ids[k, r] == e)
         return hit.astype(jnp.int32)
 
     for e in range(experts):
@@ -98,22 +101,40 @@
 
     pl.semaphore_wait(barrier, sources - 1)
 
-    @pl.loop(1, sources)
-    def _(i):
-        p = other(i)
+    for k in range(1, experts):
+        e = lax.rem(mine + k, experts)
         pltpu.make_async_remote_copy(
-            picked.at[p // per], arrived.at[me], row_send, row_recv,
-            device_id=device(p), device_id_type=pl.DeviceIdType.MESH,
+            picked.at[e], arrived.at[me], row_send, row_recv.at[mine],
+            device_id=device(e * per + spot), device_id_type=pl.DeviceIdType.MESH,
         ).start()
 
-    pltpu.make_async_copy(picked.at[mine], arrived.at[me], row_recv).start()
+    own_rows = pltpu.make_async_copy(picked.at[mine], arrived.at[me], row_recv.at[mine])
+    own_rows.start()
+    for k in range(experts):
+        e = lax.rem(mine - k + experts, experts)
+        held_rows = arrived.at[e * per + spot]
+        if k:
+            pltpu.make_async_copy(held_rows, held_rows, row_recv.at[e]).wait()
+
+        @pl.loop(1, per)
+        def _(i):
+            pltpu.make_async_remote_copy(
+                held_rows if k else picked.at[mine], held_rows, pass_send, pass_recv,
+                device_id=device(mine * per + lax.rem(spot + i, per)),
+                device_id_type=pl.DeviceIdType.MESH,
+            ).start()
+
+    own_rows.wait()
     lane = lax.broadcasted_iota(jnp.int32, (rows, LANES), 1)
     stats[0] = jnp.full((rows, LANES), NEGATIVE, jnp.float32)
     for q in range(1, 4):
         stats[q] = jnp.zeros((rows, LANES), jnp.float32)
     for q in range(4, 8):
         stat_out[:, q, :] = jnp.zeros((rows, LANES), jnp.float32)
-    pltpu.make_async_copy(arrived, arrived, row_recv).wait()
+    passed = arrived.at[pl.ds(0, sources - experts)]
+    pltpu.make_async_copy(passed, passed, pass_recv).wait()
+    for c in range(early, slots):
+        fetch(c, c).start()
     wide[...] = arrived[...].astype(jnp.float32).reshape(wide.shape)
     for k in range(depth // LANES):
         lhs[:, k * LANES:(k + 1) * LANES] = wide[:, k, :].astype(jnp.bfloat16)
@@ -178,8 +199,9 @@
     pltpu.make_async_copy(
         stat_out.at[pl.ds(MOST * me, MOST)], stat_in.at[me], stat_recv
     ).start()
-    gone_rows = arrived.at[pl.ds(0, sources - 1)]
+    gone_rows = arrived.at[pl.ds(0, experts - 1)]
     pltpu.make_async_copy(gone_rows, gone_rows, row_send).wait()
+    pltpu.make_async_copy(passed, passed, pass_send).wait()
     pltpu.make_async_copy(stat_in, stat_in, stat_recv).wait()
     for e in range(experts):
         for m in range(MOST):
@@ -198,18 +220,18 @@
         r = jnp.int32(0)
         for other_row in range(block):
             r = jnp.where(target[other_row] == t, other_row, r)
-        code_total = codes[r, 0]
+        code_total = codes[0, r]
         for k in range(1, topk):
-            code_total = code_total + codes[r, k]
+            code_total = code_total + codes[k, r]
         code_total = jnp.full((1, LANES), code_total, jnp.int32).astype(jnp.float32)
         named = []
         for k in range(topk):
-            e = ids[r, k]
+            e = ids[k, r]
             m = jnp.int32(0)
             for other_row in range(block):
                 m = m + jnp.where(other_row < r, names(other_row, e), 0)
             m = jnp.minimum(m, MOST - 1)
-            share = jnp.full((1, LANES), codes[r, k], jnp.int32).astype(jnp.float32) / code_total
+            share = jnp.full((1, LANES), codes[k, r], jnp.int32).astype(jnp.float32) / code_total
             named.append((e, m, jnp.log(share)))
 
         @pl.loop(0, per)
@@ -225,8 +247,9 @@
                     tile = landed[g, source].astype(jnp.int32).astype(jnp.float32)
                     tile = jnp.where(m == 0, tile[:tall], tile[tall:])
                     scores.append(tile * step[:, g:g + 1] + offset[:, g:g + 1])
-                peak = functools.reduce(jnp.maximum, scores)
-                summed = sum(jnp.exp(score - peak) for score in scores)
+                first, second = scores
+                peak = jnp.maximum(first, second)
+                summed = 1.0 + jnp.exp(jnp.minimum(first, second) - peak)
                 place = pl.multiple_of((j * groups + g) * tall, tall)
                 out[pl.ds(place, tall), t, :] = peak + jnp.log(summed)
 
@@ -269,6 +292,8 @@
         pltpu.SemaphoreType.DMA((3,)),
         pltpu.SemaphoreType.DMA((slots,)),
         pltpu.SemaphoreType.DMA,
+        pltpu.SemaphoreType.DMA((experts,)),
+        pltpu.SemaphoreType.DMA,
         pltpu.SemaphoreType.DMA,
         pltpu.SemaphoreType.DMA((groups,)),
         pltpu.SemaphoreType.DMA((groups,)),
@@ -291,7 +316,7 @@
             bytes_accessed=2 * depth * width,
             transcendentals=3 * rows * width,
         ),
-    )(expert_ids, weight_codes, target_rows, hidden_rows, norm_gain, norm_bias, head_weight)
+    )(expert_ids.T, weight_codes.T, target_rows, hidden_rows, norm_gain, norm_bias, head_weight)
     return jnp.transpose(mixed, (1, 0, 2)).reshape(block, per * width)
 
 

time: 58.1 us -> 46 us (0.79)
  Pallas kernels: 53.3 us -> 44 us
  local copies, waits for them, and re-layouts: 4.55 us -> 1.87 us
    pallas_call x1, Pallas kernels: 53.3 us -> 44 us  [local(): pl.pallas_call(functools.partial(kernel, experts), out_shape=jax.ShapeDty...]
    unnamed x3 -> x1, local copies, waits for them, and re-layouts: 4.55 us -> 1.87 us
where the time goes in v2:
time: 46 us; the launch traced here: 45.8 us
  Pallas kernels  44 us (96%)
  local copies, waits for them, and re-layouts  1.87 us (4%)
    pallas_call x1, Pallas kernels, local(): pl.pallas_call(functools.partial(kernel, experts), out_shape=jax.ShapeDty...  44 us
    unnamed x1, local copies, waits for them, and re-layouts  1.87 us

profile of v2, /device:TPU:0, one launch (start us, length us, event | category | flops | bytes accessed | tf_op | source)
XLA Modules:
  0.0 45.8 jit_solution(11569624315477588162)
XLA Ops:
  0.0 44.0 %shard_map.73 = f32[256,4,128]{2,1,0:T(4,128)} custom-call(s32[2,4]{1,0:T(2,128)} %bitcast.6, s32[2,4]{1,0:T(2,128)} %bitcast.7, s32[4]{0:T(128)} %target.1, bf16[4,4096]{1,0:T(4,128)(2,1)} %hidden.1, f32[4,4096]{1,0:T(4,128)} %gain.1, f32[4,4096]{1,0:T(4,128)} %bias.1, bf16[4096,8192]{1,0:T(8,128)(2,1)} %weight.1), custom_call_target="tpu_custom_call" | custom-call | flops 2147483648 | bytes 67108864 | tf_op jit(solution)/shard_map/pallas_call | solution.py:305
  44.0 1.9 %copy.9 = f32[4,32768]{1,0:T(4,128)} copy(f32[4,32768]{1,0:T(4,128)} %bitcast.5) | data formatting | bytes 1048576
